TPU v7x, 32 devices: a whole 2x2x4 slice. The times are simulated.
32 devices in a mesh: gx: 4 (over x, core), gy: 8 (over z, y).
Axes of the slice: x: 2, y: 2, z: 4, core: 2. Of those that a mesh axis runs over, the one named last changes fastest.
Arguments:
- velocity: float32 [3, 32, 32, 128], P(None, 'gx', 'gy'), may hold values from -6 to 6
- stress: float32 [6, 32, 32, 128], P(None, 'gx', 'gy'), may hold values from -6 to 6
- memory: float32 [6, 32, 32, 128], P(None, 'gx', 'gy'), may hold values from -3 to 3
- buoyancy: float32 [32, 32, 128], P('gx', 'gy'), may hold values from 0.5 to 1.5
- lame_lambda: float32 [32, 32, 128], P('gx', 'gy'), may hold values from 0.5 to 1.5
- shear_modulus: float32 [32, 32, 128], P('gx', 'gy'), may hold values from 0.3 to 1
- relaxation: float32 [32, 32, 128], P('gx', 'gy'), may hold values from 0.05 to 0.4
- surface_history: bfloat16 [32, 32, 3, 1020], P('gx', 'gy'), may hold values from -6 to 6
- site_owner: int32 [4, 8, 8, 4, 1], P('gx', 'gy'), may hold values from 0 to 7; in each aligned block of 32 rows (0 to 31, 32 to 63, ..., all dimensions but the last counted through in order) at most 8 rows name the same one
- periods: float32 [100], replicated, may hold values from 3 to 300
Outputs:
- final_velocity: float32 [3, 32, 32, 128], P(None, 'gx', 'gy')
- final_stress: float32 [6, 32, 32, 128], P(None, 'gx', 'gy')
- final_memory: float32 [6, 32, 32, 128], P(None, 'gx', 'gy')
- block_energy: float32 [4, 8, 3, 400], P('gx', 'gy')
Inputs may be any that keep to these rules, and one draw needn't show every extreme that they name: `site_owner`: among the 32 sites of one device no site block is named more than 8 times, and some block is named exactly 8 times.
All inputs are finite; a program needn't handle non-finite values.
Results may differ from a plain program's by a relative error of at most 0.001.
Values may be sent and summed in bfloat16 or wider, within the bound.
A program may use at most 64 MiB of HBM per device.

v0:
```python
import math

import jax
import jax.numpy as jnp
from jax import lax
from jax.sharding import PartitionSpec as P

ITERS = 4


TIME_STEP = 0.25
DAMPING = 0.05
RELAX = math.exp(-0.25 / 8.0)


def with_halo(cells, sides, width):
    for axis, dim in sides:
        count = lax.axis_size(axis)
        ends = count - 1
        head = lax.slice_in_dim(cells, 0, width, axis=dim)
        tail = lax.slice_in_dim(cells, cells.shape[dim] - width, cells.shape[dim], axis=dim)
        cells = jnp.concatenate(
            [
                lax.ppermute(tail, axis, [(i, (i + 1) % count) for i in range(ends)]),
                cells,
                lax.ppermute(head, axis, [((i + 1) % count, i) for i in range(ends)]),
            ],
            axis=dim,
        )
    return cells


def oscillator_table(periods, hist, iters):
    count_periods = periods.shape[0]
    span = iters * count_periods
    omega = (2.0 * math.pi / jnp.tile(periods, iters))[None, :]
    damped = omega * math.sqrt(1.0 - DAMPING * DAMPING)
    width = hist + iters
    rows = jnp.arange(width, dtype=jnp.int32)[:, None]
    step_of = (jnp.arange(span, dtype=jnp.int32) // count_periods)[None, :]
    lag = hist + step_of - rows
    valid = (lag >= 0) & (lag <= hist)
    lagf = jnp.clip(lag, 0, hist).astype(jnp.float32)
    value = omega * jnp.exp(-DAMPING * omega * lagf) * jnp.sin(damped * lagf) / damped
    return jnp.where(valid, value, 0.0).astype(jnp.bfloat16)


def horizontal(padded, comp, axis):
    if axis == 0:
        return 0.5 * (padded[comp, 2:, 1:-1, :] - padded[comp, :-2, 1:-1, :])
    return 0.5 * (padded[comp, 1:-1, 2:, :] - padded[comp, 1:-1, :-2, :])


def vertical(field):
    padded = jnp.pad(field, ((0, 0), (0, 0), (1, 1)))
    return 0.5 * (padded[:, :, 2:] - padded[:, :, :-2])


def on_device(
    velocity,
    stress,
    memory,
    buoyancy,
    lame_lambda,
    shear_modulus,
    relaxation,
    surface_history,
    site_owner,
    periods,
):
    samples = []
    for step in range(ITERS):
        stress_pad = with_halo(stress, (("gx", 1), ("gy", 2)), 1)
        force_x = horizontal(stress_pad, 0, 0) + horizontal(stress_pad, 3, 1) + vertical(stress[4])
        force_y = horizontal(stress_pad, 3, 0) + horizontal(stress_pad, 1, 1) + vertical(stress[5])
        force_z = horizontal(stress_pad, 4, 0) + horizontal(stress_pad, 5, 1) + vertical(stress[2])
        velocity = velocity + TIME_STEP * buoyancy * jnp.stack([force_x, force_y, force_z])
        moving = with_halo(velocity, (("gx", 1), ("gy", 2)), 1)
        strain_xx = horizontal(moving, 0, 0)
        strain_yy = horizontal(moving, 1, 1)
        strain_zz = vertical(velocity[2])
        strain_xy = 0.5 * (horizontal(moving, 0, 1) + horizontal(moving, 1, 0))
        strain_xz = 0.5 * (vertical(velocity[0]) + horizontal(moving, 2, 0))
        strain_yz = 0.5 * (vertical(velocity[1]) + horizontal(moving, 2, 1))
        trace = strain_xx + strain_yy + strain_zz
        elastic = jnp.stack(
            [
                lame_lambda * trace + 2.0 * shear_modulus * strain_xx,
                lame_lambda * trace + 2.0 * shear_modulus * strain_yy,
                lame_lambda * trace + 2.0 * shear_modulus * strain_zz,
                2.0 * shear_modulus * strain_xy,
                2.0 * shear_modulus * strain_xz,
                2.0 * shear_modulus * strain_yz,
            ]
        )
        memory = RELAX * memory + (1.0 - RELAX) * relaxation * elastic
        stress = stress + TIME_STEP * (elastic - memory)
        samples.append(velocity[:, :, :, 0].astype(jnp.bfloat16))
    hist = surface_history.shape[3]
    width = hist + ITERS
    sites = surface_history.shape[0] * surface_history.shape[1]
    count_periods = periods.shape[0]
    span = ITERS * count_periods
    table = oscillator_table(periods, hist, ITERS)
    fresh = jnp.transpose(jnp.stack(samples), (2, 3, 1, 0))
    window = jnp.concatenate([surface_history, fresh], axis=3).reshape(sites, 3 * width)
    blocks = lax.axis_size("gy")
    owners = site_owner.reshape(sites)
    onehot_int = (owners[:, None] == jnp.arange(blocks, dtype=jnp.int32)[None, :]).astype(jnp.int32)
    capacity = max(2, 2 * sites // blocks)
    before = jnp.cumsum(onehot_int, axis=0) - onehot_int
    rank = jnp.sum(before * onehot_int, axis=1)
    slot_index = owners * capacity + rank
    select = (
        slot_index[None, :] == jnp.arange(blocks * capacity, dtype=jnp.int32)[:, None]
    ).astype(jnp.bfloat16)
    outgoing = jnp.dot(select, window, preferred_element_type=jnp.float32).astype(jnp.bfloat16)
    outgoing = outgoing.reshape(blocks, capacity, 3, width)
    received = lax.all_to_all(outgoing, "gy", split_axis=0, concat_axis=0, tiled=True)
    sources = received.shape[0]
    items = received.shape[1]
    response = jnp.dot(received.reshape(-1, width), table, preferred_element_type=jnp.float32)
    power = response * response
    powers = power.reshape(sources, items, 3, span)
    energy = (jnp.sum(powers, axis=(0, 1)) / sites).reshape(1, 1, 3, span)
    return (velocity, stress, memory, energy)


def solution(mesh):
    in_specs = (
        P(None, "gx", "gy", None),
        P(None, "gx", "gy", None),
        P(None, "gx", "gy", None),
        P("gx", "gy", None),
        P("gx", "gy", None),
        P("gx", "gy", None),
        P("gx", "gy", None),
        P("gx", "gy", None, None),
        P("gx", "gy", None, None, None),
        P(),
    )
    out_specs = (
        P(None, "gx", "gy", None),
        P(None, "gx", "gy", None),
        P(None, "gx", "gy", None),
        P("gx", "gy", None, None),
    )
    return jax.shard_map(
        on_device, mesh=mesh, in_specs=in_specs, out_specs=out_specs, check_vma=False
    )
```

profile of v0, /device:TPU:6, one launch (start us, length us, event | category | flops | bytes accessed | tf_op | source)
XLA Modules:
  0.0 154.9 jit_solution(18190690926944206127)
XLA Ops:
  3.3 3.6 %collective-permute-start = (f32[6,1,4,128]{3,2,1,0:T(4,128)S(1)}, f32[6,1,4,128]{3,2,1,0:T(4,128)S(1)}, u32[]{:S(2)}, u32[]{:S(2)}) collective-permute-start(f32[6,1,4,128]{3,2,1,0:T(4,128)S(1)} %get-tuple-element.51), channel_id=1, source_target_pairs={{8,0},{16,8},{24,16},{9,1},{17,9},{25,17},{10,2},{18,10},{26,18},{... | collective-permute-start | bytes 36872 | tf_op jit(solution)/shard_map/ppermute | solution.py:26
  9.5 3.4 %collective-permute-start.3 = (f32[6,10,1,128]{3,2,1,0:T(1,128)S(1)}, f32[6,10,1,128]{3,2,1,0:T(1,128)S(1)}, u32[]{:S(2)}, u32[]{:S(2)}) collective-permute-start(f32[6,10,1,128]{3,2,1,0:T(1,128)S(1)} %get-tuple-element.29), channel_id=1, source_target_pairs={{0,1},{1,2},{2,3},{3,4},{4,5},{5,6},{6,7},{8,9},{9,10},{10,11},{11... | collective-permute-start | bytes 92168 | tf_op jit(solution)/shard_map/ppermute | solution.py:24
  13.0 2.4 %collective-permute-start.2 = (f32[6,10,1,128]{3,2,1,0:T(1,128)S(1)}, f32[6,10,1,128]{3,2,1,0:T(1,128)S(1)}, u32[]{:S(2)}, u32[]{:S(2)}) collective-permute-start(f32[6,10,1,128]{3,2,1,0:T(1,128)S(1)} %get-tuple-element.28), channel_id=1, source_target_pairs={{1,0},{2,1},{3,2},{4,3},{5,4},{6,5},{7,6},{9,8},{10,9},{11,10},{12... | collective-permute-start | bytes 92168 | tf_op jit(solution)/shard_map/ppermute | solution.py:26
  15.6 4.1 %collective-permute-done.2 = f32[6,10,1,128]{3,2,1,0:T(1,128)S(1)} collective-permute-done((f32[6,10,1,128]{3,2,1,0:T(1,128)S(1)}, f32[6,10,1,128]{3,2,1,0:T(1,128)S(1)}, u32[]{:S(2)}, u32[]{:S(2)}) %collective-permute-start.2) | collective-permute-done | bytes 30752 | tf_op jit(solution)/shard_map/ppermute | solution.py:26
  22.0 3.6 %collective-permute-start.4 = (f32[3,1,4,128]{3,2,1,0:T(4,128)S(1)}, f32[3,1,4,128]{3,2,1,0:T(4,128)S(1)}, u32[]{:S(2)}, u32[]{:S(2)}) collective-permute-start(f32[3,1,4,128]{3,2,1,0:T(4,128)S(1)} %get-tuple-element.83), channel_id=1, source_target_pairs={{8,0},{16,8},{24,16},{9,1},{17,9},{25,17},{10,2},{18,10},{26,18},{... | collective-permute-start | bytes 18440 | tf_op jit(solution)/shard_map/ppermute | solution.py:26
  27.0 2.5 %collective-permute-start.7 = (f32[3,10,1,128]{3,2,1,0:T(1,128)S(1)}, f32[3,10,1,128]{3,2,1,0:T(1,128)S(1)}, u32[]{:S(2)}, u32[]{:S(2)}) collective-permute-start(f32[3,10,1,128]{3,2,1,0:T(1,128)S(1)} %get-tuple-element.60), channel_id=1, source_target_pairs={{0,1},{1,2},{2,3},{3,4},{4,5},{5,6},{6,7},{8,9},{9,10},{10,11},{11... | collective-permute-start | bytes 46088 | tf_op jit(solution)/shard_map/ppermute | solution.py:24
  29.5 3.3 %collective-permute-start.6 = (f32[3,10,1,128]{3,2,1,0:T(1,128)S(1)}, f32[3,10,1,128]{3,2,1,0:T(1,128)S(1)}, u32[]{:S(2)}, u32[]{:S(2)}) collective-permute-start(f32[3,10,1,128]{3,2,1,0:T(1,128)S(1)} %get-tuple-element.59), channel_id=1, source_target_pairs={{1,0},{2,1},{3,2},{4,3},{5,4},{6,5},{7,6},{9,8},{10,9},{11,10},{12... | collective-permute-start | bytes 46088 | tf_op jit(solution)/shard_map/ppermute | solution.py:26
  32.9 3.2 %collective-permute-done.6 = f32[3,10,1,128]{3,2,1,0:T(1,128)S(1)} collective-permute-done((f32[3,10,1,128]{3,2,1,0:T(1,128)S(1)}, f32[3,10,1,128]{3,2,1,0:T(1,128)S(1)}, u32[]{:S(2)}, u32[]{:S(2)}) %collective-permute-start.6) | collective-permute-done | bytes 15392 | tf_op jit(solution)/shard_map/ppermute | solution.py:26
  41.1 2.7 %collective-permute-done.9 = f32[6,1,4,128]{3,2,1,0:T(4,128)S(1)} collective-permute-done((f32[6,1,4,128]{3,2,1,0:T(4,128)S(1)}, f32[6,1,4,128]{3,2,1,0:T(4,128)S(1)}, u32[]{:S(2)}, u32[]{:S(2)}) %collective-permute-start.9) | collective-permute-done | bytes 12320 | tf_op jit(solution)/shard_map/ppermute | solution.py:24
  43.9 3.4 %collective-permute-start.11 = (f32[6,10,1,128]{3,2,1,0:T(1,128)S(1)}, f32[6,10,1,128]{3,2,1,0:T(1,128)S(1)}, u32[]{:S(2)}, u32[]{:S(2)}) collective-permute-start(f32[6,10,1,128]{3,2,1,0:T(1,128)S(1)} %get-tuple-element.27), channel_id=1, source_target_pairs={{0,1},{1,2},{2,3},{3,4},{4,5},{5,6},{6,7},{8,9},{9,10},{10,11},{11... | collective-permute-start | bytes 92168 | tf_op jit(solution)/shard_map/ppermute | solution.py:24
  47.3 2.4 %collective-permute-start.10 = (f32[6,10,1,128]{3,2,1,0:T(1,128)S(1)}, f32[6,10,1,128]{3,2,1,0:T(1,128)S(1)}, u32[]{:S(2)}, u32[]{:S(2)}) collective-permute-start(f32[6,10,1,128]{3,2,1,0:T(1,128)S(1)} %get-tuple-element.26), channel_id=1, source_target_pairs={{1,0},{2,1},{3,2},{4,3},{5,4},{6,5},{7,6},{9,8},{10,9},{11,10},{12... | collective-permute-start | bytes 92168 | tf_op jit(solution)/shard_map/ppermute | solution.py:26
  49.8 4.2 %collective-permute-done.10 = f32[6,10,1,128]{3,2,1,0:T(1,128)S(1)} collective-permute-done((f32[6,10,1,128]{3,2,1,0:T(1,128)S(1)}, f32[6,10,1,128]{3,2,1,0:T(1,128)S(1)}, u32[]{:S(2)}, u32[]{:S(2)}) %collective-permute-start.10) | collective-permute-done | bytes 30752 | tf_op jit(solution)/shard_map/ppermute | solution.py:26
  56.2 3.6 %collective-permute-start.12 = (f32[3,1,4,128]{3,2,1,0:T(4,128)S(1)}, f32[3,1,4,128]{3,2,1,0:T(4,128)S(1)}, u32[]{:S(2)}, u32[]{:S(2)}) collective-permute-start(f32[3,1,4,128]{3,2,1,0:T(4,128)S(1)} %get-tuple-element.77), channel_id=1, source_target_pairs={{8,0},{16,8},{24,16},{9,1},{17,9},{25,17},{10,2},{18,10},{26,18},{... | collective-permute-start | bytes 18440 | tf_op jit(solution)/shard_map/ppermute | solution.py:26
  61.3 2.5 %collective-permute-start.15 = (f32[3,10,1,128]{3,2,1,0:T(1,128)S(1)}, f32[3,10,1,128]{3,2,1,0:T(1,128)S(1)}, u32[]{:S(2)}, u32[]{:S(2)}) collective-permute-start(f32[3,10,1,128]{3,2,1,0:T(1,128)S(1)} %get-tuple-element.58), channel_id=1, source_target_pairs={{0,1},{1,2},{2,3},{3,4},{4,5},{5,6},{6,7},{8,9},{9,10},{10,11},{11... | collective-permute-start | bytes 46088 | tf_op jit(solution)/shard_map/ppermute | solution.py:24
  63.8 3.3 %collective-permute-start.14 = (f32[3,10,1,128]{3,2,1,0:T(1,128)S(1)}, f32[3,10,1,128]{3,2,1,0:T(1,128)S(1)}, u32[]{:S(2)}, u32[]{:S(2)}) collective-permute-start(f32[3,10,1,128]{3,2,1,0:T(1,128)S(1)} %get-tuple-element.57), channel_id=1, source_target_pairs={{1,0},{2,1},{3,2},{4,3},{5,4},{6,5},{7,6},{9,8},{10,9},{11,10},{12... | collective-permute-start | bytes 46088 | tf_op jit(solution)/shard_map/ppermute | solution.py:26
  67.1 3.2 %collective-permute-done.14 = f32[3,10,1,128]{3,2,1,0:T(1,128)S(1)} collective-permute-done((f32[3,10,1,128]{3,2,1,0:T(1,128)S(1)}, f32[3,10,1,128]{3,2,1,0:T(1,128)S(1)}, u32[]{:S(2)}, u32[]{:S(2)}) %collective-permute-start.14) | collective-permute-done | bytes 15392 | tf_op jit(solution)/shard_map/ppermute | solution.py:26
  75.4 2.7 %collective-permute-done.17 = f32[6,1,4,128]{3,2,1,0:T(4,128)S(1)} collective-permute-done((f32[6,1,4,128]{3,2,1,0:T(4,128)S(1)}, f32[6,1,4,128]{3,2,1,0:T(4,128)S(1)}, u32[]{:S(2)}, u32[]{:S(2)}) %collective-permute-start.17) | collective-permute-done | bytes 12320 | tf_op jit(solution)/shard_map/ppermute | solution.py:24
  78.1 3.4 %collective-permute-start.19 = (f32[6,10,1,128]{3,2,1,0:T(1,128)S(1)}, f32[6,10,1,128]{3,2,1,0:T(1,128)S(1)}, u32[]{:S(2)}, u32[]{:S(2)}) collective-permute-start(f32[6,10,1,128]{3,2,1,0:T(1,128)S(1)} %get-tuple-element.25), channel_id=1, source_target_pairs={{0,1},{1,2},{2,3},{3,4},{4,5},{5,6},{6,7},{8,9},{9,10},{10,11},{11... | collective-permute-start | bytes 92168 | tf_op jit(solution)/shard_map/ppermute | solution.py:24
  81.6 2.4 %collective-permute-start.18 = (f32[6,10,1,128]{3,2,1,0:T(1,128)S(1)}, f32[6,10,1,128]{3,2,1,0:T(1,128)S(1)}, u32[]{:S(2)}, u32[]{:S(2)}) collective-permute-start(f32[6,10,1,128]{3,2,1,0:T(1,128)S(1)} %get-tuple-element.24), channel_id=1, source_target_pairs={{1,0},{2,1},{3,2},{4,3},{5,4},{6,5},{7,6},{9,8},{10,9},{11,10},{12... | collective-permute-start | bytes 92168 | tf_op jit(solution)/shard_map/ppermute | solution.py:26
  84.0 4.2 %collective-permute-done.18 = f32[6,10,1,128]{3,2,1,0:T(1,128)S(1)} collective-permute-done((f32[6,10,1,128]{3,2,1,0:T(1,128)S(1)}, f32[6,10,1,128]{3,2,1,0:T(1,128)S(1)}, u32[]{:S(2)}, u32[]{:S(2)}) %collective-permute-start.18) | collective-permute-done | bytes 30752 | tf_op jit(solution)/shard_map/ppermute | solution.py:26
  90.5 3.6 %collective-permute-start.20 = (f32[3,1,4,128]{3,2,1,0:T(4,128)S(1)}, f32[3,1,4,128]{3,2,1,0:T(4,128)S(1)}, u32[]{:S(2)}, u32[]{:S(2)}) collective-permute-start(f32[3,1,4,128]{3,2,1,0:T(4,128)S(1)} %get-tuple-element.71), channel_id=1, source_target_pairs={{8,0},{16,8},{24,16},{9,1},{17,9},{25,17},{10,2},{18,10},{26,18},{... | collective-permute-start | bytes 18440 | tf_op jit(solution)/shard_map/ppermute | solution.py:26
  95.5 2.5 %collective-permute-start.23 = (f32[3,10,1,128]{3,2,1,0:T(1,128)S(1)}, f32[3,10,1,128]{3,2,1,0:T(1,128)S(1)}, u32[]{:S(2)}, u32[]{:S(2)}) collective-permute-start(f32[3,10,1,128]{3,2,1,0:T(1,128)S(1)} %get-tuple-element.56), channel_id=1, source_target_pairs={{0,1},{1,2},{2,3},{3,4},{4,5},{5,6},{6,7},{8,9},{9,10},{10,11},{11... | collective-permute-start | bytes 46088 | tf_op jit(solution)/shard_map/ppermute | solution.py:24
  98.1 3.3 %collective-permute-start.22 = (f32[3,10,1,128]{3,2,1,0:T(1,128)S(1)}, f32[3,10,1,128]{3,2,1,0:T(1,128)S(1)}, u32[]{:S(2)}, u32[]{:S(2)}) collective-permute-start(f32[3,10,1,128]{3,2,1,0:T(1,128)S(1)} %get-tuple-element.55), channel_id=1, source_target_pairs={{1,0},{2,1},{3,2},{4,3},{5,4},{6,5},{7,6},{9,8},{10,9},{11,10},{12... | collective-permute-start | bytes 46088 | tf_op jit(solution)/shard_map/ppermute | solution.py:26
  101.4 3.2 %collective-permute-done.22 = f32[3,10,1,128]{3,2,1,0:T(1,128)S(1)} collective-permute-done((f32[3,10,1,128]{3,2,1,0:T(1,128)S(1)}, f32[3,10,1,128]{3,2,1,0:T(1,128)S(1)}, u32[]{:S(2)}, u32[]{:S(2)}) %collective-permute-start.22) | collective-permute-done | bytes 15392 | tf_op jit(solution)/shard_map/ppermute | solution.py:26
  114.3 3.9 %collective-permute-start.26 = (f32[6,10,1,128]{3,2,1,0:T(1,128)S(1)}, f32[6,10,1,128]{3,2,1,0:T(1,128)S(1)}, u32[]{:S(2)}, u32[]{:S(2)}) collective-permute-start(f32[6,10,1,128]{3,2,1,0:T(1,128)S(1)} %get-tuple-element.22), channel_id=1, source_target_pairs={{1,0},{2,1},{3,2},{4,3},{5,4},{6,5},{7,6},{9,8},{10,9},{11,10},{12... | collective-permute-start | bytes 92168 | tf_op jit(solution)/shard_map/ppermute | solution.py:26
  118.5 2.5 %collective-permute-done.26 = f32[6,10,1,128]{3,2,1,0:T(1,128)S(1)} collective-permute-done((f32[6,10,1,128]{3,2,1,0:T(1,128)S(1)}, f32[6,10,1,128]{3,2,1,0:T(1,128)S(1)}, u32[]{:S(2)}, u32[]{:S(2)}) %collective-permute-start.26) | collective-permute-done | bytes 30752 | tf_op jit(solution)/shard_map/ppermute | solution.py:26
  123.3 3.6 %collective-permute-start.28 = (f32[3,1,4,128]{3,2,1,0:T(4,128)S(1)}, f32[3,1,4,128]{3,2,1,0:T(4,128)S(1)}, u32[]{:S(2)}, u32[]{:S(2)}) collective-permute-start(f32[3,1,4,128]{3,2,1,0:T(4,128)S(1)} %get-tuple-element.65), channel_id=1, source_target_pairs={{8,0},{16,8},{24,16},{9,1},{17,9},{25,17},{10,2},{18,10},{26,18},{... | collective-permute-start | bytes 18440 | tf_op jit(solution)/shard_map/ppermute | solution.py:26
  128.7 4.4 %all-to-all-start = ((bf16[8,8,3,1024]{3,1,2,0:T(8,128)(2,1)}), bf16[8,8,3,1024]{3,1,2,0:T(8,128)(2,1)S(1)}, u32[]{:S(2)}, u32[]{:S(2)}) async-start(bf16[8,8,3,1024]{3,1,2,0:T(8,128)(2,1)} %bitcast.97), calls=%async_computation | async-start | bytes 786432 | tf_op jit(solution)/shard_map/all_to_all | solution.py:119
  133.2 3.4 %collective-permute-start.31 = (f32[3,10,1,128]{3,2,1,0:T(1,128)S(1)}, f32[3,10,1,128]{3,2,1,0:T(1,128)S(1)}, u32[]{:S(2)}, u32[]{:S(2)}) collective-permute-start(f32[3,10,1,128]{3,2,1,0:T(1,128)S(1)} %get-tuple-element.54), channel_id=1, source_target_pairs={{0,1},{1,2},{2,3},{3,4},{4,5},{5,6},{6,7},{8,9},{9,10},{10,11},{11... | collective-permute-start | bytes 46088 | tf_op jit(solution)/shard_map/ppermute | solution.py:24
  136.6 2.5 %collective-permute-start.30 = (f32[3,10,1,128]{3,2,1,0:T(1,128)S(1)}, f32[3,10,1,128]{3,2,1,0:T(1,128)S(1)}, u32[]{:S(2)}, u32[]{:S(2)}) collective-permute-start(f32[3,10,1,128]{3,2,1,0:T(1,128)S(1)} %get-tuple-element.53), channel_id=1, source_target_pairs={{1,0},{2,1},{3,2},{4,3},{5,4},{6,5},{7,6},{9,8},{10,9},{11,10},{12... | collective-permute-start | bytes 46088 | tf_op jit(solution)/shard_map/ppermute | solution.py:26
  139.1 4.8 %collective-permute-done.30 = f32[3,10,1,128]{3,2,1,0:T(1,128)S(1)} collective-permute-done((f32[3,10,1,128]{3,2,1,0:T(1,128)S(1)}, f32[3,10,1,128]{3,2,1,0:T(1,128)S(1)}, u32[]{:S(2)}, u32[]{:S(2)}) %collective-permute-start.30) | collective-permute-done | bytes 15392 | tf_op jit(solution)/shard_map/ppermute | solution.py:26
  145.7 8.2 %convolution_multiply_fusion = f32[192,400]{1,0:T(8,128)S(1)} fusion(bf16[192,1024]{1,0:T(8,128)(2,1)S(1)} %reshape.212, f32[400]{0:T(512)S(1)} %get-tuple-element.90, f32[400]{0:T(512)S(1)} %get-tuple-element.89, f32[400]{0:T(512)S(1)} %div.51, s32[400]{0:T(512)S(1)} %fusion.195), kind=kOutput, calls=%fused_computation.6 | convolution fusion | flops 162688000 | bytes 706816 | tf_op jit(solution)/shard_map/dot_general | solution.py:122
  (158 shorter events, 42.9 us)
Async XLA Ops:
  1.4 7.1 %collective-permute-start.1 = (f32[6,1,4,128]{3,2,1,0:T(4,128)S(1)}, f32[6,1,4,128]{3,2,1,0:T(4,128)S(1)}, u32[]{:S(2)}, u32[]{:S(2)}) collective-permute-start(f32[6,1,4,128]{3,2,1,0:T(4,128)S(1)} %get-tuple-element.52), channel_id=1, source_target_pairs={{0,8},{8,16},{16,24},{1,9},{9,17},{17,25},{2,10},{10,18},{18,26},{... | collective-permute-start | bytes 36872 | tf_op jit(solution)/shard_map/ppermute | solution.py:24
  3.3 6.1 %collective-permute-start = (f32[6,1,4,128]{3,2,1,0:T(4,128)S(1)}, f32[6,1,4,128]{3,2,1,0:T(4,128)S(1)}, u32[]{:S(2)}, u32[]{:S(2)}) collective-permute-start(f32[6,1,4,128]{3,2,1,0:T(4,128)S(1)} %get-tuple-element.51), channel_id=1, source_target_pairs={{8,0},{16,8},{24,16},{9,1},{17,9},{25,17},{10,2},{18,10},{26,18},{... | collective-permute-start | bytes 36872 | tf_op jit(solution)/shard_map/ppermute | solution.py:26
  9.5 6.1 %collective-permute-start.3 = (f32[6,10,1,128]{3,2,1,0:T(1,128)S(1)}, f32[6,10,1,128]{3,2,1,0:T(1,128)S(1)}, u32[]{:S(2)}, u32[]{:S(2)}) collective-permute-start(f32[6,10,1,128]{3,2,1,0:T(1,128)S(1)} %get-tuple-element.29), channel_id=1, source_target_pairs={{0,1},{1,2},{2,3},{3,4},{4,5},{5,6},{6,7},{8,9},{9,10},{10,11},{11... | collective-permute-start | bytes 92168 | tf_op jit(solution)/shard_map/ppermute | solution.py:24
  13.0 6.7 %collective-permute-start.2 = (f32[6,10,1,128]{3,2,1,0:T(1,128)S(1)}, f32[6,10,1,128]{3,2,1,0:T(1,128)S(1)}, u32[]{:S(2)}, u32[]{:S(2)}) collective-permute-start(f32[6,10,1,128]{3,2,1,0:T(1,128)S(1)} %get-tuple-element.28), channel_id=1, source_target_pairs={{1,0},{2,1},{3,2},{4,3},{5,4},{6,5},{7,6},{9,8},{10,9},{11,10},{12... | collective-permute-start | bytes 92168 | tf_op jit(solution)/shard_map/ppermute | solution.py:26
  19.9 5.8 %collective-permute-start.5 = (f32[3,1,4,128]{3,2,1,0:T(4,128)S(1)}, f32[3,1,4,128]{3,2,1,0:T(4,128)S(1)}, u32[]{:S(2)}, u32[]{:S(2)}) collective-permute-start(f32[3,1,4,128]{3,2,1,0:T(4,128)S(1)} %get-tuple-element.84), channel_id=1, source_target_pairs={{0,8},{8,16},{16,24},{1,9},{9,17},{17,25},{2,10},{10,18},{18,26},{... | collective-permute-start | bytes 18440 | tf_op jit(solution)/shard_map/ppermute | solution.py:24
  22.0 5.0 %collective-permute-start.4 = (f32[3,1,4,128]{3,2,1,0:T(4,128)S(1)}, f32[3,1,4,128]{3,2,1,0:T(4,128)S(1)}, u32[]{:S(2)}, u32[]{:S(2)}) collective-permute-start(f32[3,1,4,128]{3,2,1,0:T(4,128)S(1)} %get-tuple-element.83), channel_id=1, source_target_pairs={{8,0},{16,8},{24,16},{9,1},{17,9},{25,17},{10,2},{18,10},{26,18},{... | collective-permute-start | bytes 18440 | tf_op jit(solution)/shard_map/ppermute | solution.py:26
  27.0 5.9 %collective-permute-start.7 = (f32[3,10,1,128]{3,2,1,0:T(1,128)S(1)}, f32[3,10,1,128]{3,2,1,0:T(1,128)S(1)}, u32[]{:S(2)}, u32[]{:S(2)}) collective-permute-start(f32[3,10,1,128]{3,2,1,0:T(1,128)S(1)} %get-tuple-element.60), channel_id=1, source_target_pairs={{0,1},{1,2},{2,3},{3,4},{4,5},{5,6},{6,7},{8,9},{9,10},{10,11},{11... | collective-permute-start | bytes 46088 | tf_op jit(solution)/shard_map/ppermute | solution.py:24
  29.5 6.5 %collective-permute-start.6 = (f32[3,10,1,128]{3,2,1,0:T(1,128)S(1)}, f32[3,10,1,128]{3,2,1,0:T(1,128)S(1)}, u32[]{:S(2)}, u32[]{:S(2)}) collective-permute-start(f32[3,10,1,128]{3,2,1,0:T(1,128)S(1)} %get-tuple-element.59), channel_id=1, source_target_pairs={{1,0},{2,1},{3,2},{4,3},{5,4},{6,5},{7,6},{9,8},{10,9},{11,10},{12... | collective-permute-start | bytes 46088 | tf_op jit(solution)/shard_map/ppermute | solution.py:26
  38.8 5.0 %collective-permute-start.9 = (f32[6,1,4,128]{3,2,1,0:T(4,128)S(1)}, f32[6,1,4,128]{3,2,1,0:T(4,128)S(1)}, u32[]{:S(2)}, u32[]{:S(2)}) collective-permute-start(f32[6,1,4,128]{3,2,1,0:T(4,128)S(1)} %get-tuple-element.43), channel_id=1, source_target_pairs={{0,8},{8,16},{16,24},{1,9},{9,17},{17,25},{2,10},{10,18},{18,26},{... | collective-permute-start | bytes 36872 | tf_op jit(solution)/shard_map/ppermute | solution.py:24
  43.9 5.9 %collective-permute-start.11 = (f32[6,10,1,128]{3,2,1,0:T(1,128)S(1)}, f32[6,10,1,128]{3,2,1,0:T(1,128)S(1)}, u32[]{:S(2)}, u32[]{:S(2)}) collective-permute-start(f32[6,10,1,128]{3,2,1,0:T(1,128)S(1)} %get-tuple-element.27), channel_id=1, source_target_pairs={{0,1},{1,2},{2,3},{3,4},{4,5},{5,6},{6,7},{8,9},{9,10},{10,11},{11... | collective-permute-start | bytes 92168 | tf_op jit(solution)/shard_map/ppermute | solution.py:24
  47.3 6.7 %collective-permute-start.10 = (f32[6,10,1,128]{3,2,1,0:T(1,128)S(1)}, f32[6,10,1,128]{3,2,1,0:T(1,128)S(1)}, u32[]{:S(2)}, u32[]{:S(2)}) collective-permute-start(f32[6,10,1,128]{3,2,1,0:T(1,128)S(1)} %get-tuple-element.26), channel_id=1, source_target_pairs={{1,0},{2,1},{3,2},{4,3},{5,4},{6,5},{7,6},{9,8},{10,9},{11,10},{12... | collective-permute-start | bytes 92168 | tf_op jit(solution)/shard_map/ppermute | solution.py:26
  54.3 5.6 %collective-permute-start.13 = (f32[3,1,4,128]{3,2,1,0:T(4,128)S(1)}, f32[3,1,4,128]{3,2,1,0:T(4,128)S(1)}, u32[]{:S(2)}, u32[]{:S(2)}) collective-permute-start(f32[3,1,4,128]{3,2,1,0:T(4,128)S(1)} %get-tuple-element.78), channel_id=1, source_target_pairs={{0,8},{8,16},{16,24},{1,9},{9,17},{17,25},{2,10},{10,18},{18,26},{... | collective-permute-start | bytes 18440 | tf_op jit(solution)/shard_map/ppermute | solution.py:24
  56.2 5.0 %collective-permute-start.12 = (f32[3,1,4,128]{3,2,1,0:T(4,128)S(1)}, f32[3,1,4,128]{3,2,1,0:T(4,128)S(1)}, u32[]{:S(2)}, u32[]{:S(2)}) collective-permute-start(f32[3,1,4,128]{3,2,1,0:T(4,128)S(1)} %get-tuple-element.77), channel_id=1, source_target_pairs={{8,0},{16,8},{24,16},{9,1},{17,9},{25,17},{10,2},{18,10},{26,18},{... | collective-permute-start | bytes 18440 | tf_op jit(solution)/shard_map/ppermute | solution.py:26
  61.3 5.9 %collective-permute-start.15 = (f32[3,10,1,128]{3,2,1,0:T(1,128)S(1)}, f32[3,10,1,128]{3,2,1,0:T(1,128)S(1)}, u32[]{:S(2)}, u32[]{:S(2)}) collective-permute-start(f32[3,10,1,128]{3,2,1,0:T(1,128)S(1)} %get-tuple-element.58), channel_id=1, source_target_pairs={{0,1},{1,2},{2,3},{3,4},{4,5},{5,6},{6,7},{8,9},{9,10},{10,11},{11... | collective-permute-start | bytes 46088 | tf_op jit(solution)/shard_map/ppermute | solution.py:24
  63.8 6.5 %collective-permute-start.14 = (f32[3,10,1,128]{3,2,1,0:T(1,128)S(1)}, f32[3,10,1,128]{3,2,1,0:T(1,128)S(1)}, u32[]{:S(2)}, u32[]{:S(2)}) collective-permute-start(f32[3,10,1,128]{3,2,1,0:T(1,128)S(1)} %get-tuple-element.57), channel_id=1, source_target_pairs={{1,0},{2,1},{3,2},{4,3},{5,4},{6,5},{7,6},{9,8},{10,9},{11,10},{12... | collective-permute-start | bytes 46088 | tf_op jit(solution)/shard_map/ppermute | solution.py:26
  70.9 4.5 %collective-permute-start.16 = (f32[6,1,4,128]{3,2,1,0:T(4,128)S(1)}, f32[6,1,4,128]{3,2,1,0:T(4,128)S(1)}, u32[]{:S(2)}, u32[]{:S(2)}) collective-permute-start(f32[6,1,4,128]{3,2,1,0:T(4,128)S(1)} %get-tuple-element.39), channel_id=1, source_target_pairs={{8,0},{16,8},{24,16},{9,1},{17,9},{25,17},{10,2},{18,10},{26,18},{... | collective-permute-start | bytes 36872 | tf_op jit(solution)/shard_map/ppermute | solution.py:26
  73.1 5.0 %collective-permute-start.17 = (f32[6,1,4,128]{3,2,1,0:T(4,128)S(1)}, f32[6,1,4,128]{3,2,1,0:T(4,128)S(1)}, u32[]{:S(2)}, u32[]{:S(2)}) collective-permute-start(f32[6,1,4,128]{3,2,1,0:T(4,128)S(1)} %get-tuple-element.38), channel_id=1, source_target_pairs={{0,8},{8,16},{16,24},{1,9},{9,17},{17,25},{2,10},{10,18},{18,26},{... | collective-permute-start | bytes 36872 | tf_op jit(solution)/shard_map/ppermute | solution.py:24
  78.1 5.9 %collective-permute-start.19 = (f32[6,10,1,128]{3,2,1,0:T(1,128)S(1)}, f32[6,10,1,128]{3,2,1,0:T(1,128)S(1)}, u32[]{:S(2)}, u32[]{:S(2)}) collective-permute-start(f32[6,10,1,128]{3,2,1,0:T(1,128)S(1)} %get-tuple-element.25), channel_id=1, source_target_pairs={{0,1},{1,2},{2,3},{3,4},{4,5},{5,6},{6,7},{8,9},{9,10},{10,11},{11... | collective-permute-start | bytes 92168 | tf_op jit(solution)/shard_map/ppermute | solution.py:24
  81.6 6.7 %collective-permute-start.18 = (f32[6,10,1,128]{3,2,1,0:T(1,128)S(1)}, f32[6,10,1,128]{3,2,1,0:T(1,128)S(1)}, u32[]{:S(2)}, u32[]{:S(2)}) collective-permute-start(f32[6,10,1,128]{3,2,1,0:T(1,128)S(1)} %get-tuple-element.24), channel_id=1, source_target_pairs={{1,0},{2,1},{3,2},{4,3},{5,4},{6,5},{7,6},{9,8},{10,9},{11,10},{12... | collective-permute-start | bytes 92168 | tf_op jit(solution)/shard_map/ppermute | solution.py:26
  88.6 5.6 %collective-permute-start.21 = (f32[3,1,4,128]{3,2,1,0:T(4,128)S(1)}, f32[3,1,4,128]{3,2,1,0:T(4,128)S(1)}, u32[]{:S(2)}, u32[]{:S(2)}) collective-permute-start(f32[3,1,4,128]{3,2,1,0:T(4,128)S(1)} %get-tuple-element.72), channel_id=1, source_target_pairs={{0,8},{8,16},{16,24},{1,9},{9,17},{17,25},{2,10},{10,18},{18,26},{... | collective-permute-start | bytes 18440 | tf_op jit(solution)/shard_map/ppermute | solution.py:24
  90.5 5.0 %collective-permute-start.20 = (f32[3,1,4,128]{3,2,1,0:T(4,128)S(1)}, f32[3,1,4,128]{3,2,1,0:T(4,128)S(1)}, u32[]{:S(2)}, u32[]{:S(2)}) collective-permute-start(f32[3,1,4,128]{3,2,1,0:T(4,128)S(1)} %get-tuple-element.71), channel_id=1, source_target_pairs={{8,0},{16,8},{24,16},{9,1},{17,9},{25,17},{10,2},{18,10},{26,18},{... | collective-permute-start | bytes 18440 | tf_op jit(solution)/shard_map/ppermute | solution.py:26
  95.5 5.9 %collective-permute-start.23 = (f32[3,10,1,128]{3,2,1,0:T(1,128)S(1)}, f32[3,10,1,128]{3,2,1,0:T(1,128)S(1)}, u32[]{:S(2)}, u32[]{:S(2)}) collective-permute-start(f32[3,10,1,128]{3,2,1,0:T(1,128)S(1)} %get-tuple-element.56), channel_id=1, source_target_pairs={{0,1},{1,2},{2,3},{3,4},{4,5},{5,6},{6,7},{8,9},{9,10},{10,11},{11... | collective-permute-start | bytes 46088 | tf_op jit(solution)/shard_map/ppermute | solution.py:24
  98.1 6.5 %collective-permute-start.22 = (f32[3,10,1,128]{3,2,1,0:T(1,128)S(1)}, f32[3,10,1,128]{3,2,1,0:T(1,128)S(1)}, u32[]{:S(2)}, u32[]{:S(2)}) collective-permute-start(f32[3,10,1,128]{3,2,1,0:T(1,128)S(1)} %get-tuple-element.55), channel_id=1, source_target_pairs={{1,0},{2,1},{3,2},{4,3},{5,4},{6,5},{7,6},{9,8},{10,9},{11,10},{12... | collective-permute-start | bytes 46088 | tf_op jit(solution)/shard_map/ppermute | solution.py:26
  105.1 4.9 %collective-permute-start.24 = (f32[6,1,4,128]{3,2,1,0:T(4,128)S(1)}, f32[6,1,4,128]{3,2,1,0:T(4,128)S(1)}, u32[]{:S(2)}, u32[]{:S(2)}) collective-permute-start(f32[6,1,4,128]{3,2,1,0:T(4,128)S(1)} %get-tuple-element.34), channel_id=1, source_target_pairs={{8,0},{16,8},{24,16},{9,1},{17,9},{25,17},{10,2},{18,10},{26,18},{... | collective-permute-start | bytes 36872 | tf_op jit(solution)/shard_map/ppermute | solution.py:26
  107.3 5.0 %collective-permute-start.25 = (f32[6,1,4,128]{3,2,1,0:T(4,128)S(1)}, f32[6,1,4,128]{3,2,1,0:T(4,128)S(1)}, u32[]{:S(2)}, u32[]{:S(2)}) collective-permute-start(f32[6,1,4,128]{3,2,1,0:T(4,128)S(1)} %get-tuple-element.33), channel_id=1, source_target_pairs={{0,8},{8,16},{16,24},{1,9},{9,17},{17,25},{2,10},{10,18},{18,26},{... | collective-permute-start | bytes 36872 | tf_op jit(solution)/shard_map/ppermute | solution.py:24
  112.4 6.1 %collective-permute-start.27 = (f32[6,10,1,128]{3,2,1,0:T(1,128)S(1)}, f32[6,10,1,128]{3,2,1,0:T(1,128)S(1)}, u32[]{:S(2)}, u32[]{:S(2)}) collective-permute-start(f32[6,10,1,128]{3,2,1,0:T(1,128)S(1)} %get-tuple-element.23), channel_id=1, source_target_pairs={{0,1},{1,2},{2,3},{3,4},{4,5},{5,6},{6,7},{8,9},{9,10},{10,11},{11... | collective-permute-start | bytes 92168 | tf_op jit(solution)/shard_map/ppermute | solution.py:24
  114.3 6.7 %collective-permute-start.26 = (f32[6,10,1,128]{3,2,1,0:T(1,128)S(1)}, f32[6,10,1,128]{3,2,1,0:T(1,128)S(1)}, u32[]{:S(2)}, u32[]{:S(2)}) collective-permute-start(f32[6,10,1,128]{3,2,1,0:T(1,128)S(1)} %get-tuple-element.22), channel_id=1, source_target_pairs={{1,0},{2,1},{3,2},{4,3},{5,4},{6,5},{7,6},{9,8},{10,9},{11,10},{12... | collective-permute-start | bytes 92168 | tf_op jit(solution)/shard_map/ppermute | solution.py:26
  121.4 11.8 %collective-permute-start.29 = (f32[3,1,4,128]{3,2,1,0:T(4,128)S(1)}, f32[3,1,4,128]{3,2,1,0:T(4,128)S(1)}, u32[]{:S(2)}, u32[]{:S(2)}) collective-permute-start(f32[3,1,4,128]{3,2,1,0:T(4,128)S(1)} %get-tuple-element.66), channel_id=1, source_target_pairs={{0,8},{8,16},{16,24},{1,9},{9,17},{17,25},{2,10},{10,18},{18,26},{... | collective-permute-start | bytes 18440 | tf_op jit(solution)/shard_map/ppermute | solution.py:24
  123.3 9.8 %collective-permute-start.28 = (f32[3,1,4,128]{3,2,1,0:T(4,128)S(1)}, f32[3,1,4,128]{3,2,1,0:T(4,128)S(1)}, u32[]{:S(2)}, u32[]{:S(2)}) collective-permute-start(f32[3,1,4,128]{3,2,1,0:T(4,128)S(1)} %get-tuple-element.65), channel_id=1, source_target_pairs={{8,0},{16,8},{24,16},{9,1},{17,9},{25,17},{10,2},{18,10},{26,18},{... | collective-permute-start | bytes 18440 | tf_op jit(solution)/shard_map/ppermute | solution.py:26
  128.7 16.4 %all-to-all-start = ((bf16[8,8,3,1024]{3,1,2,0:T(8,128)(2,1)}), bf16[8,8,3,1024]{3,1,2,0:T(8,128)(2,1)S(1)}, u32[]{:S(2)}, u32[]{:S(2)}) async-start(bf16[8,8,3,1024]{3,1,2,0:T(8,128)(2,1)} %bitcast.97), calls=%async_computation | async-start | bytes 786432 | tf_op jit(solution)/shard_map/all_to_all | solution.py:119
  133.2 5.9 %collective-permute-start.31 = (f32[3,10,1,128]{3,2,1,0:T(1,128)S(1)}, f32[3,10,1,128]{3,2,1,0:T(1,128)S(1)}, u32[]{:S(2)}, u32[]{:S(2)}) collective-permute-start(f32[3,10,1,128]{3,2,1,0:T(1,128)S(1)} %get-tuple-element.54), channel_id=1, source_target_pairs={{0,1},{1,2},{2,3},{3,4},{4,5},{5,6},{6,7},{8,9},{9,10},{10,11},{11... | collective-permute-start | bytes 46088 | tf_op jit(solution)/shard_map/ppermute | solution.py:24
  136.6 7.3 %collective-permute-start.30 = (f32[3,10,1,128]{3,2,1,0:T(1,128)S(1)}, f32[3,10,1,128]{3,2,1,0:T(1,128)S(1)}, u32[]{:S(2)}, u32[]{:S(2)}) collective-permute-start(f32[3,10,1,128]{3,2,1,0:T(1,128)S(1)} %get-tuple-element.53), channel_id=1, source_target_pairs={{1,0},{2,1},{3,2},{4,3},{5,4},{6,5},{7,6},{9,8},{10,9},{11,10},{12... | collective-permute-start | bytes 46088 | tf_op jit(solution)/shard_map/ppermute | solution.py:26
  (11 other events, 145.4 us)
where the time goes:
time: 156 us; the launch traced here: 155 us
  starting transfers between devices  92.1 us (59%)
  waiting for transfers between devices  41.2 us (26%)
  matrix products  9.26 us (6%)
  other arithmetic  5.45 us (3%)
  local copies, waits for them, and re-layouts  5.41 us (3%)
    ppermute x16, starting transfers between devices, with_halo(): lax.ppermute(head, axis, [((i + 1) % count, i) for i in range(ends)])  48.3 us
    ppermute x16, starting transfers between devices, with_halo(): lax.ppermute(tail, axis, [(i, (i + 1) % count) for i in range(ends)])  39.3 us
    ppermute x16, waiting for transfers between devices, with_halo(): lax.ppermute(head, axis, [((i + 1) % count, i) for i in range(ends)])  33.2 us
    dot_general x1, matrix products, on_device(): jnp.dot(received.reshape(-1, width), table, preferred_element_type=jnp.fl...  8.25 us
    ppermute x16, waiting for transfers between devices, with_halo(): lax.ppermute(tail, axis, [(i, (i + 1) % count) for i in range(ends)])  8.02 us
    all_to_all x1, starting transfers between devices, on_device(): lax.all_to_all(outgoing, 'gy', split_axis=0, concat_axis=0, tiled=True)  4.45 us
  transfers between devices with their start and end apart: 33, of which 15 were waited for; matrix products, arithmetic and copies ran while one was open for 4% of the time, Pallas kernels for 0%

commit v1 on v0

v1 whole, which is shorter than its diff:
```python
import functools
import math

import jax
import jax.numpy as jnp
from jax import lax
from jax.experimental import pallas as pl
from jax.experimental.pallas import tpu as pltpu
from jax.sharding import PartitionSpec as P

ITERS = 4
TIME_STEP = 0.25
DAMPING = 0.05
RELAX = math.exp(-0.25 / 8.0)
MESH = pl.DeviceIdType.MESH

ROWS = 96
NEAR = (0, 1, 2, 3, 4, 5, 6, 7, 8)
FAR_X = (0, 3, 4)
FAR_Y = (1, 3, 5)
WAYS = ((-1, 0), (1, 0), (0, -1), (0, 1), (-1, -1), (-1, 1), (1, -1), (1, 1))


def kernel(
    nx, ny, count_p,
    v_in, s_in, m_in, b_in, l_in, g_in, r_in, hist, owner, per,
    v_out, s_out, m_out, e_out,
    ext, bext, mem, coef, xs, xr, ys, yr, cs, cr, hi, lo, table, acc, fresh, msg, got,
    send_sem, recv_sem, esend_sem, erecv_sem,
):
    ix = lax.axis_index("gx")
    iy = lax.axis_index("gy")

    def exists(dx, dy):
        ok = None
        for at, d, n in ((ix, dx, nx), (iy, dy, ny)):
            if d:
                one = at + d >= 0 if d < 0 else at + d < n
                ok = one if ok is None else jnp.logical_and(ok, one)
        return ok

    barrier = pltpu.get_barrier_semaphore()
    total = ny - 1
    for dx, dy in WAYS:
        if dx:
            here = exists(dx, dy)
            total = total + here.astype(jnp.int32)

            @pl.when(here)
            def _():
                pl.semaphore_signal(barrier, inc=1, device_id=(ix + dx, iy + dy), device_id_type=MESH)

    def greet(i, carry):
        pl.semaphore_signal(barrier, inc=1, device_id=(ix, lax.rem(iy + i, ny)), device_id_type=MESH)
        return carry

    lax.fori_loop(1, ny, greet, 0)

    ext[...] = jnp.zeros_like(ext)
    bext[...] = jnp.zeros_like(bext)
    mem[...] = jnp.zeros_like(mem)
    coef[...] = jnp.zeros_like(coef)
    fresh[...] = jnp.zeros_like(fresh)
    for y in range(4):
        for c in range(6):
            ext[pl.ds(c * ROWS + 18 + y, 8, stride=8), :] = s_in[pl.ds(c * 32 + y, 8, stride=4), :]
        for c in range(3):
            ext[pl.ds((6 + c) * ROWS + 18 + y, 8, stride=8), :] = v_in[pl.ds(c * 32 + y, 8, stride=4), :]
        bext[pl.ds(18 + y, 8, stride=8), :] = b_in[pl.ds(y, 8, stride=4), :]

    def copy_of(step, way):
        dx, dy = WAYS[way]
        if dx and dy:
            src, dst = cs.at[step, way - 4], cr.at[step, way - 4]
        elif dx:
            src, dst = xs.at[step, way], xr.at[step, way]
        else:
            src, dst = ys.at[step, way - 2], yr.at[step, way - 2]
        if not (dx and dy) and step > 0:
            src, dst = src.at[pl.ds(0, 12)], dst.at[pl.ds(0, 12)]
        return pltpu.make_async_remote_copy(
            src_ref=src, dst_ref=dst,
            send_sem=send_sem.at[step, way], recv_sem=recv_sem.at[step, way],
            device_id=(ix + dx, iy + dy), device_id_type=MESH,
        )

    def pack(step):
        for way, (dx, dy) in enumerate(WAYS):
            if dx and dy:
                cell = (2 if dx < 0 else 9) * 8 + (2 if dy < 0 else 5)
                cs[step, way - 4] = ext[pl.ds(cell, 8, stride=ROWS), :]
            elif dx:
                near, far = (2, 3) if dx < 0 else (9, 8)
                for k, c in enumerate(NEAR):
                    xs[step, way, k] = ext[c * ROWS + near * 8:c * ROWS + near * 8 + 8, :]
                for k, c in enumerate(FAR_X):
                    xs[step, way, 9 + k] = ext[c * ROWS + far * 8:c * ROWS + far * 8 + 8, :]
                if step == 0:
                    xs[step, way, 12] = bext[near * 8:near * 8 + 8, :]
            else:
                near, far = (2, 3) if dy < 0 else (5, 4)
                for k, c in enumerate(NEAR):
                    ys[step, way - 2, k] = ext[pl.ds(c * ROWS + 16 + near, 8, stride=8), :]
                for k, c in enumerate(FAR_Y):
                    ys[step, way - 2, 9 + k] = ext[pl.ds(c * ROWS + 16 + far, 8, stride=8), :]
                if step == 0:
                    ys[step, way - 2, 12] = bext[pl.ds(16 + near, 8, stride=8), :]

    def start(step):
        for way in (4, 5, 6, 7, 2, 3, 0, 1):
            @pl.when(exists(*WAYS[way]))
            def _():
                copy_of(step, way).start()

    def land(step):
        for way, (dx, dy) in enumerate(WAYS):
            @pl.when(exists(-dx, -dy))
            def _():
                copy_of(step, way).wait_recv()
                if dx and dy:
                    cell = (10 if dx < 0 else 1) * 8 + (6 if dy < 0 else 1)
                    ext[pl.ds(cell, 6, stride=ROWS), :] = cr[step, way - 4, 0:6, :]
                elif dx:
                    near, far = (10, 11) if dx < 0 else (1, 0)
                    for k, c in enumerate(NEAR):
                        ext[c * ROWS + near * 8:c * ROWS + near * 8 + 8, :] = xr[step, way, k]
                    for k, c in enumerate(FAR_X):
                        ext[c * ROWS + far * 8:c * ROWS + far * 8 + 8, :] = xr[step, way, 9 + k]
                    if step == 0:
                        bext[near * 8:near * 8 + 8, :] = xr[step, way, 12]
                else:
                    near, far = (6, 7) if dy < 0 else (1, 0)
                    for k, c in enumerate(NEAR):
                        ext[pl.ds(c * ROWS + 16 + near, 8, stride=8), :] = yr[step, way - 2, k]
                    for k, c in enumerate(FAR_Y):
                        ext[pl.ds(c * ROWS + 16 + far, 8, stride=8), :] = yr[step, way - 2, 9 + k]
                    if step == 0:
                        bext[pl.ds(16 + near, 8, stride=8), :] = yr[step, way - 2, 12]

    lane = lax.broadcasted_iota(jnp.int32, (1, 1, 128), 2)

    def diff_x(f):
        return f[2:] - f[:-2]

    def diff_y(f):
        return pltpu.roll(f, 7, 1) - pltpu.roll(f, 1, 1)

    def diff_z(f):
        above = jnp.where(lane == 127, 0.0, pltpu.roll(f, 127, 2))
        below = jnp.where(lane == 0, 0.0, pltpu.roll(f, 1, 2))
        return above - below

    def field(c, first, last):
        return ext[c * ROWS + first * 8:c * ROWS + last * 8, :].reshape(last - first, 8, 128)

    def move(step):
        s = [field(c, 0, 12) for c in range(6)]
        push = bext[8:88, :].reshape(10, 8, 128) * (0.5 * TIME_STEP)
        forces = (
            diff_x(s[0]) + diff_y(s[3][1:11]) + diff_z(s[4][1:11]),
            diff_x(s[3]) + diff_y(s[1][1:11]) + diff_z(s[5][1:11]),
            diff_x(s[4]) + diff_y(s[5][1:11]) + diff_z(s[2][1:11]),
        )
        for c in range(3):
            v = field(6 + c, 1, 11) + push * forces[c]
            ext[(6 + c) * ROWS + 8:(6 + c) * ROWS + 88, :] = v.reshape(80, 128)
            top = jnp.where(lane == 128 - ITERS + step, v[1:9, :, 0:1], 0.0).reshape(64, 128)
            fresh[c * 64:c * 64 + 64, :] = fresh[c * 64:c * 64 + 64, :] + top

    def strain(step):
        v = [field(6 + c, 1, 11) for c in range(3)]
        mid = [f[1:9] for f in v]
        lam, mu, rel = (coef[k].reshape(8, 8, 128) for k in range(3))
        xx, yy, zz = diff_x(v[0]) * 0.5, diff_y(mid[1]) * 0.5, diff_z(mid[2]) * 0.5
        trace = lam * (xx + yy + zz)
        twice = 2.0 * mu
        half = 0.5 * mu
        rates = (
            trace + twice * xx,
            trace + twice * yy,
            trace + twice * zz,
            half * (diff_y(mid[0]) + diff_x(v[1])),
            half * (diff_z(mid[0]) + diff_x(v[2])),
            half * (diff_z(mid[1]) + diff_y(mid[2])),
        )
        gain = (1.0 - RELAX) * rel
        for c in range(6):
            m = RELAX * mem[c].reshape(8, 8, 128) + gain * rates[c]
            mem[c] = m.reshape(64, 128)
            s = field(c, 2, 10) + TIME_STEP * (rates[c] - m)
            ext[c * ROWS + 16:c * ROWS + 80, :] = s.reshape(64, 128)

    span = hi.shape[2]
    q = lax.broadcasted_iota(jnp.int32, (1, span), 1)
    step_of = jnp.zeros((1, span), jnp.int32)
    for t in range(1, ITERS):
        step_of = step_of + (q >= t * count_p).astype(jnp.int32)
    width = table.shape[0]
    length = width - ITERS

    def powers():
        omega = (2.0 * math.pi) / per[...]
        damped = omega * math.sqrt(1.0 - DAMPING * DAMPING)
        row = lax.broadcasted_iota(jnp.int32, (32, span), 0)
        low = (31 - row).astype(jnp.float32)
        high = (length - 31 + step_of - 32 * row).astype(jnp.float32)
        size = jnp.exp(-DAMPING * omega * low)
        lo[0] = size * jnp.cos(damped * low)
        lo[1] = size * jnp.sin(damped * low)
        size = jnp.exp(-DAMPING * omega * high) * (omega / damped)
        hi[0] = size * jnp.sin(damped * high)
        hi[1] = size * jnp.cos(damped * high)

    def fill():
        def one(a, carry):
            value = hi[0, pl.ds(a, 1), :] * lo[0] + hi[1, pl.ds(a, 1), :] * lo[1]
            row = lax.broadcasted_iota(jnp.int32, (32, span), 0) + 32 * a
            lag = length + step_of - row
            valid = jnp.logical_and(lag >= 0, lag <= length)
            table[pl.ds(pl.multiple_of(a * 32, 32), 32), :] = jnp.where(valid, value, 0.0).astype(jnp.bfloat16)
            return carry

        lax.fori_loop(0, width // 32, one, 0)

    def history():
        acc[...] = jnp.dot(hist[...], table[...], preferred_element_type=jnp.float32)

    pack(0)
    pl.semaphore_wait(barrier, total)
    start(0)
    for y in range(4):
        for c in range(6):
            mem[c, pl.ds(2 + y, 8, stride=8), :] = m_in[pl.ds(c * 32 + y, 8, stride=4), :]
        for k, ref in enumerate((l_in, g_in, r_in)):
            coef[k, pl.ds(2 + y, 8, stride=8), :] = ref[pl.ds(y, 8, stride=4), :]
    powers()
    for step in range(ITERS):
        land(step)
        move(step)
        if step < ITERS - 1:
            strain(step)
            pack(step + 1)
            start(step + 1)
            if step == 0:
                fill()
            if step == 1:
                history()

    rows = [fresh[pl.ds(c * 64 + 2 + y, 8, stride=8), :] for c in range(3) for y in range(4)]
    recent = jnp.concatenate(rows, axis=0).astype(jnp.bfloat16)
    response = acc[...] + jnp.dot(recent, table[width - 128:, :], preferred_element_type=jnp.float32)
    power = response * response
    sites = owner.shape[1]
    flat = jnp.concatenate([power[c * sites:(c + 1) * sites] for c in range(3)], axis=1)
    onehot = jnp.where(lax.broadcasted_iota(jnp.int32, (ny, sites), 0) == owner[...], 1.0, 0.0)
    sums = jnp.dot(onehot, flat, precision=lax.Precision.HIGHEST, preferred_element_type=jnp.float32) * (1.0 / sites)
    for o in range(ny):
        msg[o] = sums[o:o + 1, :]

    def energy_copy(i):
        to = lax.rem(iy + i, ny)
        return pltpu.make_async_remote_copy(
            src_ref=msg.at[to], dst_ref=got.at[i],
            send_sem=esend_sem.at[i], recv_sem=erecv_sem.at[i],
            device_id=(ix, to), device_id_type=MESH,
        )

    def send_energy(i, carry):
        energy_copy(i).start()
        return carry

    lax.fori_loop(1, ny, send_energy, 0)

    strain(ITERS - 1)
    for y in range(4):
        for c in range(6):
            s_out[pl.ds(c * 32 + y, 8, stride=4), :] = ext[pl.ds(c * ROWS + 18 + y, 8, stride=8), :]
            m_out[pl.ds(c * 32 + y, 8, stride=4), :] = mem[c, pl.ds(2 + y, 8, stride=8), :]
        for c in range(3):
            v_out[pl.ds(c * 32 + y, 8, stride=4), :] = ext[pl.ds((6 + c) * ROWS + 18 + y, 8, stride=8), :]
    for step in range(ITERS):
        for way in range(8):
            @pl.when(exists(*WAYS[way]))
            def _():
                copy_of(step, way).wait_send()

    def take(i, energy):
        energy_copy(i).wait()
        return energy + got[i]

    energy = lax.fori_loop(1, ny, take, msg[iy])
    for c in range(3):
        e_out[c:c + 1, :] = energy[:, c * span:c * span + e_out.shape[1]]


def solution(mesh):
    nx, ny = mesh.shape["gx"], mesh.shape["gy"]

    def on_device(velocity, stress, memory, buoyancy, lame_lambda, shear_modulus, relaxation,
                  surface_history, site_owner, periods):
        _, cx, cy, cz = velocity.shape
        sites = cx * cy
        length = surface_history.shape[3]
        width = length + ITERS
        count_p = periods.shape[0]
        cols = ITERS * count_p
        span = -(-cols // 128) * 128
        hist = jnp.transpose(surface_history, (2, 1, 0, 3)).reshape(3 * sites, length)
        hist = jnp.pad(hist, ((0, 0), (0, ITERS)))
        owner = jnp.transpose(site_owner.reshape(cx, cy)).reshape(1, sites)
        per = jnp.pad(jnp.tile(periods, ITERS), (0, span - cols), constant_values=3.0)[None, :]
        f32 = jnp.float32
        vmem = pl.BlockSpec(memory_space=pltpu.VMEM)
        out = pl.pallas_call(
            functools.partial(kernel, nx, ny, count_p),
            out_shape=(
                jax.ShapeDtypeStruct((3 * sites, cz), f32),
                jax.ShapeDtypeStruct((6 * sites, cz), f32),
                jax.ShapeDtypeStruct((6 * sites, cz), f32),
                jax.ShapeDtypeStruct((3, cols), f32),
            ),
            in_specs=[vmem] * 10,
            out_specs=(vmem,) * 4,
            scratch_shapes=[
                pltpu.VMEM((9 * ROWS, cz), f32),
                pltpu.VMEM((ROWS, cz), f32),
                pltpu.VMEM((6, 64, cz), f32),
                pltpu.VMEM((3, 64, cz), f32),
                pltpu.VMEM((ITERS, 2, 13, 8, cz), f32),
                pltpu.VMEM((ITERS, 2, 13, 8, cz), f32),
                pltpu.VMEM((ITERS, 2, 13, 8, cz), f32),
                pltpu.VMEM((ITERS, 2, 13, 8, cz), f32),
                pltpu.VMEM((ITERS, 4, 8, cz), f32),
                pltpu.VMEM((ITERS, 4, 8, cz), f32),
                pltpu.VMEM((2, 32, span), f32),
                pltpu.VMEM((2, 32, span), f32),
                pltpu.VMEM((width, span), jnp.bfloat16),
                pltpu.VMEM((3 * sites, span), f32),
                pltpu.VMEM((3 * 64, cz), f32),
                pltpu.VMEM((ny, 1, 3 * span), f32),
                pltpu.VMEM((ny, 1, 3 * span), f32),
                pltpu.SemaphoreType.DMA((ITERS, 8)),
                pltpu.SemaphoreType.DMA((ITERS, 8)),
                pltpu.SemaphoreType.DMA((ny,)),
                pltpu.SemaphoreType.DMA((ny,)),
            ],
            compiler_params=pltpu.CompilerParams(
                collective_id=0, has_side_effects=True, vmem_limit_bytes=32 * 1024 * 1024
            ),
        )(
            velocity.reshape(3 * sites, cz), stress.reshape(6 * sites, cz), memory.reshape(6 * sites, cz),
            buoyancy.reshape(sites, cz), lame_lambda.reshape(sites, cz), shear_modulus.reshape(sites, cz),
            relaxation.reshape(sites, cz), hist, owner, per,
        )
        return (
            out[0].reshape(3, cx, cy, cz), out[1].reshape(6, cx, cy, cz), out[2].reshape(6, cx, cy, cz),
            out[3].reshape(1, 1, 3, cols),
        )

    field4 = P(None, "gx", "gy", None)
    field3 = P("gx", "gy", None)
    return jax.shard_map(
        on_device, mesh=mesh,
        in_specs=(field4, field4, field4, field3, field3, field3, field3,
                  P("gx", "gy", None, None), P("gx", "gy", None, None, None), P()),
        out_specs=(field4, field4, field4, P("gx", "gy", None, None)),
        check_vma=False,
    )
```

time: 156 us -> 34.3 us (0.22)
  the two profiles are of different devices: /device:TPU:6 before, /device:TPU:0 now
where the time goes in v1:
time: 34.3 us; the launch traced here: 34.1 us
  Pallas kernels  27.5 us (80%)
  local copies, waits for them, and re-layouts  5.8 us (17%)
  between operations  0.73 us (2%)
    pallas_call x1, Pallas kernels, on_device(): pl.pallas_call(functools.partial(kernel, nx, ny, count_p), out_shape=(jax...  27.5 us
    unnamed x22, local copies, waits for them, and re-layouts  4.62 us
    transpose x1, local copies, waits for them, and re-layouts, on_device(): jnp.transpose(surface_history, (2, 1, 0, 3)).reshape(3 * sites, length)  0.99 us

profile of v1, /device:TPU:0, one launch (start us, length us, event | category | flops | bytes accessed | tf_op | source)
XLA Modules:
  0.0 34.1 jit_solution(127110102581955987)
XLA Ops:
  0.6 0.0 copy-start.7
  0.6 0.7 %copy-done.7 = s32[1,1,8,4,1]{2,4,3,1,0:T(1,128)S(1)} copy-done((s32[1,1,8,4,1]{2,4,3,1,0:T(1,128)S(1)}, s32[1,1,8,4,1]{2,4,3,1,0:T(1,128)}, u32[]{:S(2)}) %copy-start.7) | copy-done | bytes 152
  1.3 0.0 copy-start.8
  1.3 0.1 reshape.60.owner
  1.4 0.6 %copy-done.8 = f32[100]{0:T(128)S(1)} copy-done((f32[100]{0:T(128)S(1)}, f32[100]{0:T(128)}, u32[]{:S(2)}) %copy-start.8) | copy-done | bytes 424
  2.0 0.1 tile.10
  2.1 1.0 %copy.14 = bf16[3,4,8,1020]{3,2,1,0:T(8,128)(2,1)S(1)} copy(bf16[3,4,8,1020]{3,1,0,2:T(4,128)(2,1)} %bitcast.30) | data formatting | bytes 391680 | tf_op jit(solution)/shard_map/transpose | solution.py:308
  3.1 0.0 copy-start
  3.1 0.0 copy-start.1
  3.1 0.0 copy-start.2
  3.1 0.0 copy-start.3
  3.1 0.0 copy-start.4
  3.1 0.0 copy-start.5
  3.1 0.0 copy-start.6
  3.2 0.8 %copy-done = f32[6,8,4,128]{3,2,1,0:T(4,128)S(1)} copy-done((f32[6,8,4,128]{3,2,1,0:T(4,128)S(1)}, f32[6,8,4,128]{3,2,1,0:T(4,128)}, u32[]{:S(2)}) %copy-start) | copy-done | bytes 98328
  4.0 0.0 copy-done.1
  4.0 0.0 copy-done.2
  4.0 0.0 copy-done.3
  4.0 0.0 copy-done.4
  4.0 0.0 copy-done.5
  4.0 0.0 copy-done.6
  4.0 27.5 %shard_map.129 = (f32[96,128]{1,0:T(8,128)S(1)}, f32[192,128]{1,0:T(8,128)S(1)}, f32[192,128]{1,0:T(8,128)S(1)}, f32[3,400]{1,0:T(4,128)S(1)}) custom-call(f32[96,128]{1,0:T(8,128)S(1)} %bitcast.21, f32[192,128]{1,0:T(8,128)S(1)} %bitcast.17, f32[192,128]{1,0:T(8,128)S(1)} %bitcast.18, f32[32,128]{1,0:T(8,128)S(1)} %bitcast.23, f32[32,128]{1,0:T(8,128)S(1)} %bitcast.24, ...), custom_call_target="tpu_custom_call" | custom-call | tf_op jit(solution)/shard_map/pallas_call | solution.py:314
  31.6 0.6 %copy.15 = f32[1,1,3,400]{3,1,2,0:T(1,128)} copy(f32[1,1,3,400]{3,2,1,0:T(4,128)S(1)} %bitcast.28) | data formatting | bytes 9600
  32.2 0.6 %copy.19 = f32[3,8,4,128]{3,2,1,0:T(4,128)} copy(f32[3,8,4,128]{3,2,1,0:T(4,128)S(1)} %bitcast.22) | data formatting | bytes 98304
  32.8 0.6 %copy.20 = f32[6,8,4,128]{3,2,1,0:T(4,128)} copy(f32[6,8,4,128]{3,2,1,0:T(4,128)S(1)} %bitcast.20) | data formatting | bytes 196608
  33.4 0.6 %copy.21 = f32[6,8,4,128]{3,2,1,0:T(4,128)} copy(f32[6,8,4,128]{3,2,1,0:T(4,128)S(1)} %bitcast.19) | data formatting | bytes 196608
  (3 shorter events, 0.0 us)
Async XLA Ops:
  0.6 0.7 %copy-start.7 = (s32[1,1,8,4,1]{2,4,3,1,0:T(1,128)S(1)}, s32[1,1,8,4,1]{2,4,3,1,0:T(1,128)}, u32[]{:S(2)}) copy-start(s32[1,1,8,4,1]{2,4,3,1,0:T(1,128)} %param.18) | copy-start | bytes 388
  1.3 0.7 %copy-start.8 = (f32[100]{0:T(128)S(1)}, f32[100]{0:T(128)}, u32[]{:S(2)}) copy-start(f32[100]{0:T(128)} %param.19) | copy-start | bytes 1204
  3.1 0.9 %copy-start = (f32[6,8,4,128]{3,2,1,0:T(4,128)S(1)}, f32[6,8,4,128]{3,2,1,0:T(4,128)}, u32[]{:S(2)}) copy-start(f32[6,8,4,128]{3,2,1,0:T(4,128)} %param.11) | copy-start | bytes 294916
  3.1 0.9 %copy-start.1 = (f32[6,8,4,128]{3,2,1,0:T(4,128)S(1)}, f32[6,8,4,128]{3,2,1,0:T(4,128)}, u32[]{:S(2)}) copy-start(f32[6,8,4,128]{3,2,1,0:T(4,128)} %param.12) | copy-start | bytes 294916
  3.1 0.9 %copy-start.2 = (f32[3,8,4,128]{3,2,1,0:T(4,128)S(1)}, f32[3,8,4,128]{3,2,1,0:T(4,128)}, u32[]{:S(2)}) copy-start(f32[3,8,4,128]{3,2,1,0:T(4,128)} %param.10) | copy-start | bytes 147460
  3.1 0.9 %copy-start.3 = (f32[8,4,128]{2,1,0:T(4,128)S(1)}, f32[8,4,128]{2,1,0:T(4,128)}, u32[]{:S(2)}) copy-start(f32[8,4,128]{2,1,0:T(4,128)} %param.13) | copy-start | bytes 49156
  3.1 0.9 %copy-start.4 = (f32[8,4,128]{2,1,0:T(4,128)S(1)}, f32[8,4,128]{2,1,0:T(4,128)}, u32[]{:S(2)}) copy-start(f32[8,4,128]{2,1,0:T(4,128)} %param.14) | copy-start | bytes 49156
  3.1 0.9 %copy-start.5 = (f32[8,4,128]{2,1,0:T(4,128)S(1)}, f32[8,4,128]{2,1,0:T(4,128)}, u32[]{:S(2)}) copy-start(f32[8,4,128]{2,1,0:T(4,128)} %param.15) | copy-start | bytes 49156
  3.1 0.9 %copy-start.6 = (f32[8,4,128]{2,1,0:T(4,128)S(1)}, f32[8,4,128]{2,1,0:T(4,128)}, u32[]{:S(2)}) copy-start(f32[8,4,128]{2,1,0:T(4,128)} %param.16) | copy-start | bytes 49156

commit v2 on v1

--- a/solution.py
+++ b/solution.py
@@ -15,18 +15,19 @@
 MESH = pl.DeviceIdType.MESH
 
 ROWS = 96
-NEAR = (0, 1, 2, 3, 4, 5, 6, 7, 8)
-FAR_X = (0, 3, 4)
-FAR_Y = (1, 3, 5)
+BY_X = (0, 3, 4)
+BY_Y = (3, 1, 5)
+BY_Z = (4, 5, 2)
 WAYS = ((-1, 0), (1, 0), (0, -1), (0, 1), (-1, -1), (-1, 1), (1, -1), (1, 1))
 
 
 def kernel(
     nx, ny, count_p,
-    v_in, s_in, m_in, b_in, l_in, g_in, r_in, hist, owner, per,
+    v_hbm, s_hbm, m_hbm, b_hbm, l_hbm, g_hbm, r_hbm, hist_hbm, owner_hbm, per_hbm,
     v_out, s_out, m_out, e_out,
-    ext, bext, mem, coef, xs, xr, ys, yr, cs, cr, hi, lo, table, acc, fresh, msg, got,
-    send_sem, recv_sem, esend_sem, erecv_sem,
+    v_in, s_in, m_in, b_in, l_in, g_in, r_in, hist_in, owner, per_in,
+    ext, bext, mem, coef, xs, xr, ys, yr, cs, cr, hist, per, hi, lo, table, acc, fresh, late, msg, got,
+    load_sem, send_sem, recv_sem, esend_sem, erecv_sem,
 ):
     ix = lax.axis_index("gx")
     iy = lax.axis_index("gy")
@@ -39,6 +40,19 @@
                 ok = one if ok is None else jnp.logical_and(ok, one)
         return ok
 
+    loads = [
+        pltpu.make_async_copy(src, dst, load_sem.at[i])
+        for i, (src, dst) in enumerate((
+            (s_hbm, s_in), (v_hbm, v_in), (b_hbm, b_in), (m_hbm, m_in), (l_hbm, l_in),
+            (g_hbm, g_in), (r_hbm, r_in), (per_hbm, per_in), (hist_hbm, hist_in), (owner_hbm, owner),
+        ))
+    ]
+    for load in loads:
+        load.start()
+
+    for buf in (xr, yr, cr):
+        buf[...] = jnp.zeros_like(buf)
+
     barrier = pltpu.get_barrier_semaphore()
     total = ny - 1
     for dx, dy in WAYS:
@@ -61,6 +75,8 @@
     mem[...] = jnp.zeros_like(mem)
     coef[...] = jnp.zeros_like(coef)
     fresh[...] = jnp.zeros_like(fresh)
+    for load in loads[:3]:
+        load.wait()
     for y in range(4):
         for c in range(6):
             ext[pl.ds(c * ROWS + 18 + y, 8, stride=8), :] = s_in[pl.ds(c * 32 + y, 8, stride=4), :]
@@ -77,12 +93,34 @@
         else:
             src, dst = ys.at[step, way - 2], yr.at[step, way - 2]
         if not (dx and dy) and step > 0:
-            src, dst = src.at[pl.ds(0, 12)], dst.at[pl.ds(0, 12)]
+            count = 3 if dx else 6
+            src, dst = src.at[pl.ds(0, count)], dst.at[pl.ds(0, count)]
         return pltpu.make_async_remote_copy(
             src_ref=src, dst_ref=dst,
             send_sem=send_sem.at[step, way], recv_sem=recv_sem.at[step, way],
             device_id=(ix + dx, iy + dy), device_id_type=MESH,
         )
+
+    lane = lax.broadcasted_iota(jnp.int32, (1, 128), 1)
+    sub = lax.broadcasted_iota(jnp.int32, (8, 1), 0)
+    push_by = 0.5 * TIME_STEP
+
+    def diff_z(f):
+        axis = f.ndim - 1
+        above = jnp.where(lane == 127, 0.0, pltpu.roll(f, 127, axis))
+        below = jnp.where(lane == 0, 0.0, pltpu.roll(f, 1, axis))
+        return above - below
+
+    def x_tile(c, x):
+        return ext[c * ROWS + (x + 2) * 8:c * ROWS + (x + 2) * 8 + 8, :]
+
+    def y_tile(c, y):
+        return ext[pl.ds(c * ROWS + 18 + y, 8, stride=8), :]
+
+    def inside(f, first, last):
+        above = jnp.where(sub == last, 0.0, pltpu.roll(f, 7, 0))
+        below = jnp.where(sub == first, 0.0, pltpu.roll(f, 1, 0))
+        return above - below
 
     def pack(step):
         for way, (dx, dy) in enumerate(WAYS):
@@ -90,21 +128,24 @@
                 cell = (2 if dx < 0 else 9) * 8 + (2 if dy < 0 else 5)
                 cs[step, way - 4] = ext[pl.ds(cell, 8, stride=ROWS), :]
             elif dx:
-                near, far = (2, 3) if dx < 0 else (9, 8)
-                for k, c in enumerate(NEAR):
-                    xs[step, way, k] = ext[c * ROWS + near * 8:c * ROWS + near * 8 + 8, :]
-                for k, c in enumerate(FAR_X):
-                    xs[step, way, 9 + k] = ext[c * ROWS + far * 8:c * ROWS + far * 8 + 8, :]
+                near, far, sign = (0, 1, 1.0) if dx < 0 else (7, 6, -1.0)
+                push = bext[(near + 2) * 8:(near + 2) * 8 + 8, :]
+                keep = jnp.logical_and(sub >= 2, sub < 6)
+                for c in range(3):
+                    force = sign * x_tile(BY_X[c], far) + inside(x_tile(BY_Y[c], near), 2, 5) + diff_z(x_tile(BY_Z[c], near))
+                    v = x_tile(6 + c, near) + (push_by * push) * force
+                    xs[step, way, c] = jnp.where(keep, x_tile(BY_X[c], near), pltpu.roll(v, 4, 0))
                 if step == 0:
-                    xs[step, way, 12] = bext[near * 8:near * 8 + 8, :]
+                    xs[step, way, 3] = push
             else:
-                near, far = (2, 3) if dy < 0 else (5, 4)
-                for k, c in enumerate(NEAR):
-                    ys[step, way - 2, k] = ext[pl.ds(c * ROWS + 16 + near, 8, stride=8), :]
-                for k, c in enumerate(FAR_Y):
-                    ys[step, way - 2, 9 + k] = ext[pl.ds(c * ROWS + 16 + far, 8, stride=8), :]
+                near, far, sign = (0, 1, 1.0) if dy < 0 else (3, 2, -1.0)
+                push = bext[pl.ds(18 + near, 8, stride=8), :]
+                for c in range(3):
+                    force = inside(y_tile(BY_X[c], near), 0, 7) + sign * y_tile(BY_Y[c], far) + diff_z(y_tile(BY_Z[c], near))
+                    ys[step, way - 2, c] = y_tile(BY_Y[c], near)
+                    ys[step, way - 2, 3 + c] = y_tile(6 + c, near) + (push_by * push) * force
                 if step == 0:
-                    ys[step, way - 2, 12] = bext[pl.ds(16 + near, 8, stride=8), :]
+                    ys[step, way - 2, 6] = push
 
     def start(step):
         for way in (4, 5, 6, 7, 2, 3, 0, 1):
@@ -117,27 +158,30 @@
             @pl.when(exists(-dx, -dy))
             def _():
                 copy_of(step, way).wait_recv()
-                if dx and dy:
-                    cell = (10 if dx < 0 else 1) * 8 + (6 if dy < 0 else 1)
-                    ext[pl.ds(cell, 6, stride=ROWS), :] = cr[step, way - 4, 0:6, :]
-                elif dx:
-                    near, far = (10, 11) if dx < 0 else (1, 0)
-                    for k, c in enumerate(NEAR):
-                        ext[c * ROWS + near * 8:c * ROWS + near * 8 + 8, :] = xr[step, way, k]
-                    for k, c in enumerate(FAR_X):
-                        ext[c * ROWS + far * 8:c * ROWS + far * 8 + 8, :] = xr[step, way, 9 + k]
-                    if step == 0:
-                        bext[near * 8:near * 8 + 8, :] = xr[step, way, 12]
-                else:
-                    near, far = (6, 7) if dy < 0 else (1, 0)
-                    for k, c in enumerate(NEAR):
-                        ext[pl.ds(c * ROWS + 16 + near, 8, stride=8), :] = yr[step, way - 2, k]
-                    for k, c in enumerate(FAR_Y):
-                        ext[pl.ds(c * ROWS + 16 + far, 8, stride=8), :] = yr[step, way - 2, 9 + k]
-                    if step == 0:
-                        bext[pl.ds(16 + near, 8, stride=8), :] = yr[step, way - 2, 12]
-
-    lane = lax.broadcasted_iota(jnp.int32, (1, 1, 128), 2)
+
+        for way, (dx, dy) in enumerate(WAYS[:4]):
+            if dx:
+                out, near, sign = (8, 7, -1.0) if dx < 0 else (-1, 0, 1.0)
+                push = xr[0, way, 3] * push_by
+                low, high = WAYS.index((dx, 1)) - 4, WAYS.index((dx, -1)) - 4
+                for c in range(3):
+                    both = xr[step, way, c]
+                    corner = jnp.where(sub == 2, -cr[step, low, BY_Y[c]:BY_Y[c] + 1, :], 0.0)
+                    corner = corner + jnp.where(sub == 5, cr[step, high, BY_Y[c]:BY_Y[c] + 1, :], 0.0)
+                    v = pltpu.roll(both, 4, 0) + push * (corner + sign * x_tile(BY_X[c], near))
+                    at = (out + 2) * 8
+                    ext[BY_X[c] * ROWS + at:BY_X[c] * ROWS + at + 8, :] = both
+                    ext[(6 + c) * ROWS + at:(6 + c) * ROWS + at + 8, :] = v
+            else:
+                out, near, sign = (4, 3, -1.0) if dy < 0 else (-1, 0, 1.0)
+                push = yr[0, way - 2, 6] * push_by
+                low, high = WAYS.index((1, dy)) - 4, WAYS.index((-1, dy)) - 4
+                for c in range(3):
+                    corner = jnp.where(sub == 0, -cr[step, low, BY_X[c]:BY_X[c] + 1, :], 0.0)
+                    corner = corner + jnp.where(sub == 7, cr[step, high, BY_X[c]:BY_X[c] + 1, :], 0.0)
+                    v = yr[step, way - 2, 3 + c] + push * (corner + sign * y_tile(BY_Y[c], near))
+                    ext[pl.ds(BY_Y[c] * ROWS + 18 + out, 8, stride=8), :] = yr[step, way - 2, c]
+                    ext[pl.ds((6 + c) * ROWS + 18 + out, 8, stride=8), :] = v
 
     def diff_x(f):
         return f[2:] - f[:-2]
@@ -145,26 +189,19 @@
     def diff_y(f):
         return pltpu.roll(f, 7, 1) - pltpu.roll(f, 1, 1)
 
-    def diff_z(f):
-        above = jnp.where(lane == 127, 0.0, pltpu.roll(f, 127, 2))
-        below = jnp.where(lane == 0, 0.0, pltpu.roll(f, 1, 2))
-        return above - below
-
     def field(c, first, last):
         return ext[c * ROWS + first * 8:c * ROWS + last * 8, :].reshape(last - first, 8, 128)
 
     def move(step):
-        s = [field(c, 0, 12) for c in range(6)]
-        push = bext[8:88, :].reshape(10, 8, 128) * (0.5 * TIME_STEP)
-        forces = (
-            diff_x(s[0]) + diff_y(s[3][1:11]) + diff_z(s[4][1:11]),
-            diff_x(s[3]) + diff_y(s[1][1:11]) + diff_z(s[5][1:11]),
-            diff_x(s[4]) + diff_y(s[5][1:11]) + diff_z(s[2][1:11]),
-        )
+        s = [field(c, 1, 11) for c in range(6)]
+        push = bext[16:80, :].reshape(8, 8, 128) * push_by
+        inner = jnp.logical_and(sub >= 2, sub < 6)
         for c in range(3):
-            v = field(6 + c, 1, 11) + push * forces[c]
-            ext[(6 + c) * ROWS + 8:(6 + c) * ROWS + 88, :] = v.reshape(80, 128)
-            top = jnp.where(lane == 128 - ITERS + step, v[1:9, :, 0:1], 0.0).reshape(64, 128)
+            force = diff_x(s[BY_X[c]]) + diff_y(s[BY_Y[c]][1:9]) + diff_z(s[BY_Z[c]][1:9])
+            old = field(6 + c, 2, 10)
+            v = jnp.where(inner, old + push * force, old)
+            ext[(6 + c) * ROWS + 16:(6 + c) * ROWS + 80, :] = v.reshape(64, 128)
+            top = jnp.where(lane == 128 - ITERS + step, v[:, :, 0:1], 0.0).reshape(64, 128)
             fresh[c * 64:c * 64 + 64, :] = fresh[c * 64:c * 64 + 64, :] + top
 
     def strain(step):
@@ -198,6 +235,17 @@
     width = table.shape[0]
     length = width - ITERS
 
+    def prepare():
+        cols = per_in.shape[1]
+        per[...] = jnp.full_like(per, 3.0)
+        for t in range(ITERS):
+            per[:, t * cols:(t + 1) * cols] = per_in[...]
+        hist[:, width - 128:] = jnp.zeros((hist.shape[0], 128), jnp.float32)
+        for x in range(8):
+            for c in range(3):
+                at = c * 32 + x * 4
+                hist[at:at + 4, 0:length] = hist_in[x, c].astype(jnp.float32)
+
     def powers():
         omega = (2.0 * math.pi) / per[...]
         damped = omega * math.sqrt(1.0 - DAMPING * DAMPING)
@@ -223,16 +271,19 @@
         lax.fori_loop(0, width // 32, one, 0)
 
     def history():
-        acc[...] = jnp.dot(hist[...], table[...], preferred_element_type=jnp.float32)
+        acc[...] = jnp.dot(hist[...].astype(jnp.bfloat16), table[...], preferred_element_type=jnp.float32)
 
     pack(0)
     pl.semaphore_wait(barrier, total)
     start(0)
+    for load in loads[3:]:
+        load.wait()
     for y in range(4):
         for c in range(6):
             mem[c, pl.ds(2 + y, 8, stride=8), :] = m_in[pl.ds(c * 32 + y, 8, stride=4), :]
         for k, ref in enumerate((l_in, g_in, r_in)):
             coef[k, pl.ds(2 + y, 8, stride=8), :] = ref[pl.ds(y, 8, stride=4), :]
+    prepare()
     powers()
     for step in range(ITERS):
         land(step)
@@ -246,13 +297,21 @@
             if step == 1:
                 history()
 
-    rows = [fresh[pl.ds(c * 64 + 2 + y, 8, stride=8), :] for c in range(3) for y in range(4)]
-    recent = jnp.concatenate(rows, axis=0).astype(jnp.bfloat16)
+    for c in range(3):
+        for y in range(4):
+            late[pl.ds(c * 32 + y, 8, stride=4), :] = fresh[pl.ds(c * 64 + 2 + y, 8, stride=8), :]
+    recent = late[...].astype(jnp.bfloat16)
     response = acc[...] + jnp.dot(recent, table[width - 128:, :], preferred_element_type=jnp.float32)
     power = response * response
-    sites = owner.shape[1]
+    sites = owner.shape[0] * owner.shape[1]
     flat = jnp.concatenate([power[c * sites:(c + 1) * sites] for c in range(3)], axis=1)
-    onehot = jnp.where(lax.broadcasted_iota(jnp.int32, (ny, sites), 0) == owner[...], 1.0, 0.0)
+    at_x = lax.broadcasted_iota(jnp.int32, (8, sites), 1) // 4 == lax.broadcasted_iota(jnp.int32, (8, sites), 0)
+    at_y = lax.broadcasted_iota(jnp.int32, (4, sites), 1) % 4 == lax.broadcasted_iota(jnp.int32, (4, sites), 0)
+    spread = jnp.dot(owner[...].astype(jnp.float32), jnp.where(at_x, 1.0, 0.0),
+                     precision=lax.Precision.HIGHEST, preferred_element_type=jnp.float32)
+    named = jnp.sum(jnp.where(at_y, spread, 0.0), axis=0, keepdims=True)
+    block = lax.broadcasted_iota(jnp.int32, (ny, sites), 0).astype(jnp.float32)
+    onehot = jnp.where(block == named, 1.0, 0.0)
     sums = jnp.dot(onehot, flat, precision=lax.Precision.HIGHEST, preferred_element_type=jnp.float32) * (1.0 / sites)
     for o in range(ny):
         msg[o] = sums[o:o + 1, :]
@@ -290,7 +349,20 @@
 
     energy = lax.fori_loop(1, ny, take, msg[iy])
     for c in range(3):
-        e_out[c:c + 1, :] = energy[:, c * span:c * span + e_out.shape[1]]
+        e_out[c] = energy[:, c * span:c * span + e_out.shape[2]]
+
+
+def place(*refs):
+    ins, outs, held, sem = refs[:4], refs[4:8], refs[8:12], refs[12]
+    fetch = [pltpu.make_async_copy(ins[i], held[i], sem.at[0, i]) for i in range(4)]
+    store = [pltpu.make_async_copy(held[i], outs[i], sem.at[1, i]) for i in range(4)]
+    for copy in fetch:
+        copy.start()
+    for i in range(4):
+        fetch[i].wait()
+        store[i].start()
+    for copy in store:
+        copy.wait()
 
 
 def solution(mesh):
@@ -305,10 +377,8 @@
         count_p = periods.shape[0]
         cols = ITERS * count_p
         span = -(-cols // 128) * 128
-        hist = jnp.transpose(surface_history, (2, 1, 0, 3)).reshape(3 * sites, length)
-        hist = jnp.pad(hist, ((0, 0), (0, ITERS)))
-        owner = jnp.transpose(site_owner.reshape(cx, cy)).reshape(1, sites)
-        per = jnp.pad(jnp.tile(periods, ITERS), (0, span - cols), constant_values=3.0)[None, :]
+        hist = jnp.transpose(surface_history, (0, 2, 1, 3))
+        owner = jnp.transpose(site_owner.reshape(cx, cy))
         f32 = jnp.float32
         vmem = pl.BlockSpec(memory_space=pltpu.VMEM)
         out = pl.pallas_call(
@@ -317,44 +387,66 @@
                 jax.ShapeDtypeStruct((3 * sites, cz), f32),
                 jax.ShapeDtypeStruct((6 * sites, cz), f32),
                 jax.ShapeDtypeStruct((6 * sites, cz), f32),
-                jax.ShapeDtypeStruct((3, cols), f32),
+                jax.ShapeDtypeStruct((3, 1, cols), f32),
             ),
-            in_specs=[vmem] * 10,
+            in_specs=[pl.BlockSpec(memory_space=pltpu.HBM)] * 10,
             out_specs=(vmem,) * 4,
             scratch_shapes=[
+                pltpu.VMEM((3 * sites, cz), f32),
+                pltpu.VMEM((6 * sites, cz), f32),
+                pltpu.VMEM((6 * sites, cz), f32),
+                pltpu.VMEM((sites, cz), f32),
+                pltpu.VMEM((sites, cz), f32),
+                pltpu.VMEM((sites, cz), f32),
+                pltpu.VMEM((sites, cz), f32),
+                pltpu.VMEM((cx, 3, cy, length), jnp.bfloat16),
+                pltpu.VMEM((cy, cx), jnp.int32),
+                pltpu.VMEM((1, count_p), f32),
                 pltpu.VMEM((9 * ROWS, cz), f32),
                 pltpu.VMEM((ROWS, cz), f32),
                 pltpu.VMEM((6, 64, cz), f32),
                 pltpu.VMEM((3, 64, cz), f32),
-                pltpu.VMEM((ITERS, 2, 13, 8, cz), f32),
-                pltpu.VMEM((ITERS, 2, 13, 8, cz), f32),
-                pltpu.VMEM((ITERS, 2, 13, 8, cz), f32),
-                pltpu.VMEM((ITERS, 2, 13, 8, cz), f32),
+                pltpu.VMEM((ITERS, 2, 4, 8, cz), f32),
+                pltpu.VMEM((ITERS, 2, 4, 8, cz), f32),
+                pltpu.VMEM((ITERS, 2, 7, 8, cz), f32),
+                pltpu.VMEM((ITERS, 2, 7, 8, cz), f32),
                 pltpu.VMEM((ITERS, 4, 8, cz), f32),
                 pltpu.VMEM((ITERS, 4, 8, cz), f32),
+                pltpu.VMEM((3 * sites, width), f32),
+                pltpu.VMEM((1, span), f32),
                 pltpu.VMEM((2, 32, span), f32),
                 pltpu.VMEM((2, 32, span), f32),
                 pltpu.VMEM((width, span), jnp.bfloat16),
                 pltpu.VMEM((3 * sites, span), f32),
                 pltpu.VMEM((3 * 64, cz), f32),
+                pltpu.VMEM((3 * sites, cz), f32),
                 pltpu.VMEM((ny, 1, 3 * span), f32),
                 pltpu.VMEM((ny, 1, 3 * span), f32),
+                pltpu.SemaphoreType.DMA((10,)),
                 pltpu.SemaphoreType.DMA((ITERS, 8)),
                 pltpu.SemaphoreType.DMA((ITERS, 8)),
                 pltpu.SemaphoreType.DMA((ny,)),
                 pltpu.SemaphoreType.DMA((ny,)),
             ],
             compiler_params=pltpu.CompilerParams(
-                collective_id=0, has_side_effects=True, vmem_limit_bytes=32 * 1024 * 1024
+                collective_id=0, has_side_effects=True, vmem_limit_bytes=60 * 1024 * 1024
             ),
         )(
             velocity.reshape(3 * sites, cz), stress.reshape(6 * sites, cz), memory.reshape(6 * sites, cz),
             buoyancy.reshape(sites, cz), lame_lambda.reshape(sites, cz), shear_modulus.reshape(sites, cz),
-            relaxation.reshape(sites, cz), hist, owner, per,
+            relaxation.reshape(sites, cz), hist, owner, periods[None, :],
         )
+        out = pl.pallas_call(
+            place,
+            out_shape=tuple(jax.ShapeDtypeStruct(part.shape, part.dtype) for part in out),
+            in_specs=[pl.BlockSpec(memory_space=pl.ANY)] * 4,
+            out_specs=(pl.BlockSpec(memory_space=pltpu.HBM),) * 4,
+            scratch_shapes=[pltpu.VMEM(part.shape, part.dtype) for part in out] + [pltpu.SemaphoreType.DMA((2, 4))],
+            compiler_params=pltpu.CompilerParams(vmem_limit_bytes=60 * 1024 * 1024),
+        )(*out)
         return (
             out[0].reshape(3, cx, cy, cz), out[1].reshape(6, cx, cy, cz), out[2].reshape(6, cx, cy, cz),
-            out[3].reshape(1, 1, 3, cols),
+            jnp.transpose(out[3], (1, 0, 2))[None],
         )
 
     field4 = P(None, "gx", "gy", None)

time: 34.3 us -> 28.6 us (0.83)
  local copies, waits for them, and re-layouts: 5.8 us -> 0 us
    unnamed x22 -> x0, local copies, waits for them, and re-layouts: 4.62 us -> none
    pallas_call x0 -> x1, Pallas kernels: none -> 1.68 us  [on_device(): pl.pallas_call(place, out_shape=tuple((jax.ShapeDtypeStruct(part.shape, p...]
    pallas_call x1, Pallas kernels: 27.5 us -> 26.1 us  [on_device(): pl.pallas_call(functools.partial(kernel, nx, ny, count_p), out_shape=(jax...]
    transpose x1 -> x0, local copies, waits for them, and re-layouts: 0.99 us -> none  [on_device(): jnp.transpose(surface_history, (2, 1, 0, 3)).reshape(3 * sites, length)]
where the time goes in v2:
time: 28.6 us; the launch traced here: 28.4 us
  Pallas kernels  27.7 us (97%)
  between operations  0.64 us (2%)
    pallas_call x1, Pallas kernels, on_device(): pl.pallas_call(functools.partial(kernel, nx, ny, count_p), out_shape=(jax...  26.1 us
    pallas_call x1, Pallas kernels, on_device(): pl.pallas_call(place, out_shape=tuple((jax.ShapeDtypeStruct(part.shape, p...  1.68 us

profile of v2, /device:TPU:0, one launch (start us, length us, event | category | flops | bytes accessed | tf_op | source)
XLA Modules:
  0.0 28.4 jit_solution(18105053470052350655)
XLA Ops:
  0.6 26.1 %shard_map.129 = (f32[96,128]{1,0:T(8,128)}, f32[192,128]{1,0:T(8,128)}, f32[192,128]{1,0:T(8,128)}, f32[3,1,400]{2,1,0:T(1,128)}) custom-call(f32[96,128]{1,0:T(8,128)} %bitcast.21, f32[192,128]{1,0:T(8,128)} %bitcast.19, f32[192,128]{1,0:T(8,128)} %bitcast.20, f32[32,128]{1,0:T(8,128)} %bitcast.22, f32[32,128]{1,0:T(8,128)} %bitcast.23, ...), custom_call_target="tpu_custom_call" | custom-call | tf_op jit(solution)/shard_map/pallas_call | solution.py:384
  26.7 1.7 %shard_map.130 = (f32[96,128]{1,0:T(8,128)}, f32[192,128]{1,0:T(8,128)}, f32[192,128]{1,0:T(8,128)}, f32[3,1,400]{2,1,0:T(1,128)}) custom-call(f32[96,128]{1,0:T(8,128)} %get-tuple-element.12.refs_0_, f32[192,128]{1,0:T(8,128)} %get-tuple-element.13.refs_1_, f32[192,128]{1,0:T(8,128)} %get-tuple-element.14.refs_2_, f32[3,1,400]{2,1,0:T(1,128)} %get-tuple-element.15.refs_3_), custom_call_target="tpu_custom_call" | custom-call | tf_op jit(solution)/shard_map/pallas_call | solution.py:439
